TPU v7x, 512 devices: a whole 4x8x8 slice. The times are simulated.
512 devices in a mesh: seq: 32 (over z, x), dp: 2 (over core), tensor: 8 (over y).
Axes of the slice: x: 4, y: 8, z: 8, core: 2. Of those that a mesh axis runs over, the one named last changes fastest.
Arguments:
- head_inputs: bfloat16 [2, 2560, 16384], P('dp', 'tensor', 'seq'), may hold values from -6 to 6
- b_proj: bfloat16 [2, 16384, 128], P('dp', 'seq'), may hold values from -0.59765625 to 0.59765625
- c_proj: bfloat16 [2, 16384, 128], P('dp', 'seq'), may hold values from -0.59765625 to 0.59765625
- dt_raw: float32 [2, 40, 16384], P('dp', 'tensor', 'seq'), may hold values from -2 to 0
- a_log: float32 [40], P('tensor'), as said below
- d_skip: float32 [40], P('tensor'), may hold values from 0.5 to 1.5
- w_out: bfloat16 [2560, 2560], P('tensor', 'dp'), may hold values from -0.125 to 0.125
- out_grad: bfloat16 [2, 2560, 16384], P('dp', 'tensor', 'seq'), may hold values from -6 to 6
Outputs:
- mixed: bfloat16 [2, 2560, 16384], P('dp', 'tensor', 'seq')
- grad_inputs: bfloat16 [2, 2560, 16384], P('dp', 'tensor', 'seq')
- grad_b: bfloat16 [2, 16384, 128], P('dp', 'seq')
- grad_c: bfloat16 [2, 16384, 128], P('dp', 'seq')
- grad_dt: float32 [2, 40, 16384], P('dp', 'tensor', 'seq')
- grad_alog: float32 [40], P('tensor')
- grad_skip: float32 [40], P('tensor')
- grad_w: bfloat16 [2560, 2560], P('tensor', ('seq', 'dp'))
Inputs may be any that keep to these rules, and one draw needn't show every extreme that they name: exp(a_log) lies between 0.1 / 16384 and 0.1.
All inputs are finite; a program needn't handle non-finite values.
Results may differ from a plain program's by a relative error of at most 0.0049.
Values may be sent and summed in bfloat16 or wider, within the bound.
A program may use at most 128 MiB of HBM per device.

v0:
```python
import jax
import jax.numpy as jnp
from jax import lax
from jax.sharding import PartitionSpec as P

SPAN = 256
HIGH = lax.Precision.HIGHEST


def span_pass(carried, x_block, b_block, c_block, step_block, decay_rate):
    log_decay = step_block * decay_rate[:, None]
    cumulative = jnp.cumsum(log_decay, axis=1)
    block = cumulative.shape[1]
    indices = jnp.arange(block)
    causal = (indices[:, None] >= indices[None, :])[None, :, :]
    spread = cumulative[:, :, None] - cumulative[:, None, :]
    weights = jnp.where(causal, jnp.exp(jnp.where(causal, spread, 0.0)), 0.0)
    affinity = jnp.dot(c_block, b_block.T, precision=HIGH)
    scores = affinity[None, :, :] * weights * step_block[:, None, :]
    block_out = jnp.einsum("hps,hts->hpt", x_block, scores, precision=HIGH)
    block_out = block_out + jnp.exp(cumulative)[:, None, :] * jnp.einsum(
        "hpn,tn->hpt", carried, c_block, precision=HIGH
    )
    tail_weight = jnp.exp(cumulative[:, -1:] - cumulative) * step_block
    updated = jnp.exp(cumulative[:, -1])[:, None, None] * carried
    updated = updated + jnp.einsum(
        "hps,sn->hpn", x_block * tail_weight[:, None, :], b_block, precision=HIGH
    )
    return (updated, block_out)


def sweep(streams, b_rows, c_rows, dt_rows, alog_part, skip_part, state_in):
    head_count, head_width, length = streams.shape
    blocks = length // SPAN
    step_size = jax.nn.softplus(dt_rows)
    decay_rate = -jnp.exp(alog_part)
    x_blocks = streams.reshape(head_count, head_width, blocks, SPAN).transpose(2, 0, 1, 3)
    b_blocks = b_rows.reshape(blocks, SPAN, b_rows.shape[1])
    c_blocks = c_rows.reshape(blocks, SPAN, c_rows.shape[1])
    s_blocks = step_size.reshape(head_count, blocks, SPAN).transpose(1, 0, 2)

    def advance(carried, inputs):
        return span_pass(carried, inputs[0], inputs[1], inputs[2], inputs[3], decay_rate)

    state_end, outputs = lax.scan(advance, state_in, (x_blocks, b_blocks, c_blocks, s_blocks))
    mixed_f = outputs.transpose(1, 2, 0, 3).reshape(head_count, head_width, length)
    return (mixed_f + skip_part[:, None, None] * streams, state_end)


def per_device(head_inputs, b_proj, c_proj, dt_raw, a_log, d_skip, w_out, out_grad):
    head_count = dt_raw.shape[1]
    length = head_inputs.shape[2]
    head_width = head_inputs.shape[1] // head_count
    streams = head_inputs[0].astype(jnp.float32).reshape(head_count, head_width, length)
    b_rows = b_proj[0].astype(jnp.float32)
    c_rows = c_proj[0].astype(jnp.float32)
    dt_rows = dt_raw[0]
    decay_rate = -jnp.exp(a_log)
    step_size = jax.nn.softplus(dt_rows)
    cumulative = jnp.cumsum(step_size * decay_rate[:, None], axis=1)
    device_decay = cumulative[:, -1]
    tail_weight = jnp.exp(device_decay[:, None] - cumulative) * step_size
    local_state = jnp.einsum(
        "hpt,tn->hpn", streams * tail_weight[:, None, :], b_rows, precision=HIGH
    )
    totals = lax.all_gather(device_decay[None, :], "seq", axis=0, tiled=True)
    prefix = jnp.cumsum(totals, axis=0)
    my_index = lax.axis_index("seq")
    reached = lax.dynamic_index_in_dim(prefix, my_index, 0, keepdims=False)
    before = reached - device_decay
    shard_part = lax.all_gather(local_state[None], "seq", axis=0, tiled=True)
    row_count = shard_part.shape[0]
    indices = jnp.arange(row_count, dtype=jnp.int32)
    prefix_ends = prefix
    active = (indices < my_index)[:, None]
    weights = jnp.where(active, jnp.exp(jnp.where(active, before[None, :] - prefix_ends, 0.0)), 0.0)
    state_in = jnp.einsum("jh,jhpn->hpn", weights, shard_part, precision=HIGH)

    def local_sweep(xa, ba, ca, da, aa, sa):
        return sweep(xa, ba, ca, da, aa, sa, state_in)

    primal, pullback = jax.vjp(local_sweep, streams, b_rows, c_rows, dt_rows, a_log, d_skip)
    mixed_half = primal[0].reshape(head_count * head_width, length).astype(jnp.bfloat16)
    g_full = lax.all_gather(out_grad[0], "tensor", axis=0, tiled=True)
    cotan_sum = jnp.dot(
        lax.all_gather(w_out, "dp", axis=1, tiled=True), g_full, preferred_element_type=jnp.float32
    )
    cotan_half = cotan_sum.astype(jnp.bfloat16)
    y_cotan = (
        lax.optimization_barrier(cotan_half)
        .astype(jnp.float32)
        .reshape(head_count, head_width, length)
    )
    local_cotan = jnp.einsum(
        "hpt,tn->hpn", y_cotan * jnp.exp(cumulative)[:, None, :], c_rows, precision=HIGH
    )
    shard_part = lax.all_gather(local_cotan[None], "seq", axis=0, tiled=True)
    row_count = shard_part.shape[0]
    indices = jnp.arange(row_count, dtype=jnp.int32)
    prefix_ends = prefix
    active = (indices > my_index)[:, None]
    weights = jnp.where(
        active, jnp.exp(jnp.where(active, prefix_ends - totals - reached[None, :], 0.0)), 0.0
    )
    cotan_in = jnp.einsum("jh,jhpn->hpn", weights, shard_part, precision=HIGH)
    grads = pullback((y_cotan, cotan_in))
    w_terms = lax.dot_general(
        mixed_half, g_full, (((1,), (1,)), ((), ())), preferred_element_type=jnp.float32
    )
    grad_w = lax.psum_scatter(w_terms, ("seq", "dp"), scatter_dimension=1, tiled=True).astype(
        jnp.bfloat16
    )
    grad_b, grad_c = lax.psum((grads[1], grads[2]), "tensor")
    grad_alog, grad_skip = lax.psum((grads[4], grads[5]), ("seq", "dp"))
    grad_inputs = grads[0].reshape(head_count * head_width, length).astype(jnp.bfloat16)
    return (
        mixed_half[None],
        grad_inputs[None],
        grad_b.astype(jnp.bfloat16)[None],
        grad_c.astype(jnp.bfloat16)[None],
        grads[3][None],
        grad_alog,
        grad_skip,
        grad_w,
    )


def solution(mesh):
    in_specs = (
        P("dp", "tensor", "seq"),
        P("dp", "seq", None),
        P("dp", "seq", None),
        P("dp", "tensor", "seq"),
        P("tensor"),
        P("tensor"),
        P("tensor", "dp"),
        P("dp", "tensor", "seq"),
    )
    out_specs = (
        P("dp", "tensor", "seq"),
        P("dp", "tensor", "seq"),
        P("dp", "seq", None),
        P("dp", "seq", None),
        P("dp", "tensor", "seq"),
        P("tensor"),
        P("tensor"),
        P("tensor", ("seq", "dp")),
    )
    return jax.shard_map(
        per_device, mesh=mesh, in_specs=in_specs, out_specs=out_specs, check_vma=False
    )
```

profile of v0, /device:TPU:16, one launch (start us, length us, event | category | flops | bytes accessed | tf_op | source)
XLA Modules:
  0.0 658.8 jit_solution(519363650831749236)
XLA Ops:
  10.1 1.5 reduce-window.46
  13.1 1.1 bitcast_multiply_fusion.16
  14.2 1.1 fusion.142
  15.4 17.3 %all-gather.9.cloned.1.call-done = bf16[320,2560]{1,0:T(8,128)(2,1)} async-done(((bf16[320,1280]{1,0:T(8,128)(2,1)}), bf16[320,2560]{1,0:T(8,128)(2,1)}) %all-gather.9.cloned.1.call-update) | async-done | bytes 1638416 | tf_op jit(solution)/shard_map/all_gather | solution.py:86
  32.7 47.4 %all-gather.13.cloned.1.call-done = bf16[1,2560,512]{2,1,0:T(8,128)(2,1)} async-done(((bf16[1,320,512]{2,1,0:T(8,128)(2,1)}), bf16[1,2560,512]{2,1,0:T(8,128)(2,1)}) %all-gather.13.cloned.1.call-update) | async-done | bytes 2621456 | tf_op jit(solution)/shard_map/all_gather | solution.py:84
  80.0 3.2 fusion.131
  83.4 1.1 fusion.140
  85.1 1.3 dynamic-slice
  87.3 76.9 %all-reduce.2 = f32[160]{0:T(256)S(1)} all-reduce(f32[160]{0:T(256)S(1)} %dynamic-update-slice), channel_id=2, replica_groups=mesh['seq'=32,'dp'=2,'tensor'=8] {'seq'}, use_global_device_ids=true, to_apply=%add.2 | all-reduce | flops 160 | bytes 1280
  165.0 1.3 dynamic-slice.1
  167.5 7.2 %all-gather.11.cloned.1.call-done = f32[160,64,128]{2,1,0:T(8,128)} async-done(((f32[5,64,128]{2,1,0:T(8,128)}), f32[160,64,128]{2,1,0:T(8,128)}) %all-gather.11.cloned.1.call-update) | async-done | bytes 5242896 | tf_op jit(solution)/shard_map/all_gather | solution.py:71
  174.6 7.7 %fusion.125 = f32[5,1,64,128]{3,1,2,0:T(1,128)S(1)} fusion(f32[32,5,1,1]{0,2,3,1:T(1,128)S(1)} %copy.117, f32[32,5,64,128]{3,2,1,0:T(8,128)} %bitcast.487), kind=kOutput, calls=%fused_computation.159 | convolution fusion | flops 15728640 | bytes 5407360 | tf_op jit(solution)/shard_map/jh,jhpn->hpn/dot_general | solution.py:77
  185.1 23.1 %while.75 = (s32[]{:T(128)}, f32[5,64,128]{2,1,0:T(8,128)S(1)}, f32[2,5,64,256]{3,2,1,0:T(8,128)}, f32[2,5,256,256]{3,2,1,0:T(8,128)}, f32[2,128,256]{1,2,0:T(8,...) while((s32[]{:T(128)}, f32[5,64,128]{2,1,0:T(8,128)S(1)}, ...), condition=%wide.region_6.7_spmd.clone.clone, body=%wide.region_3.6_spmd.clone.clone.sunk | while | flops 607838976 | bytes 16159797 | solution.py:45
  185.2 1.5 reduce-window.60
  187.1 1.1 bitcast_dynamic-update-slice_fusion.11
  188.2 2.8 multiply_dynamic-update-slice_fusion.4
  191.3 1.2 bitcast_dynamic-update-slice_fusion.12
  192.4 2.4 fusion.212
  196.8 1.5 reduce-window.60
  198.7 1.1 bitcast_dynamic-update-slice_fusion.11
  199.8 2.8 multiply_dynamic-update-slice_fusion.4
  202.8 1.2 bitcast_dynamic-update-slice_fusion.12
  204.0 2.4 fusion.212
  208.2 1.6 copy.110
  209.8 1.4 reshape.722
  211.3 5.4 fusion.127
  217.6 48.0 %all-gather.15.cloned.1.call-done = f32[160,64,128]{2,1,0:T(8,128)} async-done(((f32[5,64,128]{2,1,0:T(8,128)}), f32[160,64,128]{2,1,0:T(8,128)}) %all-gather.15.cloned.1.call-update) | async-done | bytes 5242896 | tf_op jit(solution)/shard_map/all_gather | solution.py:97
  265.6 7.7 %fusion.123 = f32[5,1,64,128]{3,1,2,0:T(1,128)S(1)} fusion(f32[32,5,1,1]{0,2,3,1:T(1,128)S(1)} %copy.120, f32[32,5,64,128]{3,2,1,0:T(8,128)} %bitcast.486), kind=kOutput, calls=%fused_computation.157 | convolution fusion | flops 15728640 | bytes 5407360 | tf_op jit(solution)/shard_map/jh,jhpn->hpn/dot_general | solution.py:105
  275.7 46.3 %while.76 = (s32[]{:T(128)}, f32[5]{0:T(128)S(1)}, f32[5,64,128]{2,1,0:T(8,128)S(1)}, f32[2,5,64,256]{3,2,1,0:T(8,128)}, f32[2,256,128]{2,1,0:T(8,128)}, /*index...) while((s32[]{:T(128)}, f32[5]{0:T(128)S(1)}, ...), condition=%wide.region_19.20_spmd.clone.clone, body=%wide.region_7.19_spmd.clone.clone.sunk | while | flops 1212566272 | bytes 13529267 | solution.py:45
  275.7 1.0 dynamic-slice_bitcast_fusion.8
  276.7 3.9 fusion.227
  281.6 1.0 fusion.228
  282.7 6.3 reduce-window.62
  290.2 1.9 fusion.240
  292.4 1.8 convolution_bitcast_fusion.5
  294.2 1.2 fusion.239
  295.4 3.0 fusion.238
  298.9 1.0 dynamic-slice_bitcast_fusion.8
  299.9 3.9 fusion.227
  304.8 1.0 fusion.228
  305.9 6.3 reduce-window.62
  313.4 1.9 fusion.240
  315.5 1.8 convolution_bitcast_fusion.5
  317.3 1.3 fusion.239
  318.6 3.0 fusion.238
  322.1 1.6 copy.114
  325.6 290.5 %all-reduce.8 = (f32[5]{0:T(128)}, f32[5]{0:T(128)}, bf16[320,2560]{0,1:T(8,128)(2,1)S(1)}) all-reduce(f32[5]{0:T(128)S(1)} %negate_multiply_fusion, f32[5]{0:T(128)S(1)} %reduce_sum.212, f32[320,2560]{0,1:T(8,128)} %fusion.127), channel_id=1, replica_groups=mesh['seq'=32,'dp'=2,'tensor'=8] {'seq','dp'}, use_global_device_ids=true, to_apply=%region_22.23 | all-reduce | flops 819210 | bytes 4915280 | tf_op jit(solution)/shard_map/psum | solution.py:114
  616.8 35.5 %all-reduce.9 = (bf16[512,128]{1,0:T(8,128)(2,1)}, bf16[512,128]{1,0:T(8,128)(2,1)}) all-reduce(f32[512,128]{1,0:T(8,128)S(1)} %bitcast.502, f32[512,128]{1,0:T(8,128)S(1)} %bitcast.503), channel_id=1, replica_groups=mesh['seq'=32,'dp'=2,'tensor'=8] {'tensor'}, use_global_device_ids=true, to_apply=%region_20.21 | all-reduce | flops 131072 | bytes 786432 | tf_op jit(solution)/shard_map/psum | solution.py:113
  (208 shorter events, 26.0 us)
Async XLA Ops:
  7.2 7.0 %copy-start.8 = (bf16[1,512,128]{2,1,0:T(8,128)(2,1)S(1)}, bf16[1,512,128]{2,1,0:T(8,128)(2,1)}, u32[]{:S(2)}) copy-start(bf16[1,512,128]{2,1,0:T(8,128)(2,1)} %param.13) | copy-start | bytes 393220
  7.2 25.5 %all-gather.9.cloned.1.call-start = ((), (), s32[]{:S(2)}) async-start(), calls=%async_computation | async-start | bytes 2457600 | tf_op jit(solution)/shard_map/all_gather | solution.py:86
  7.9 72.1 %all-gather.13.cloned.1.call-start = ((), (), s32[]{:S(2)}) async-start(), calls=%async_computation.2 | async-start | bytes 2949120 | tf_op jit(solution)/shard_map/all_gather | solution.py:84
  8.7 166.0 %all-gather.11.cloned.1.call-start = ((), (), s32[]{:S(2)}) async-start(), calls=%async_computation.1 | async-start | bytes 5406720 | tf_op jit(solution)/shard_map/all_gather | solution.py:71
  15.3 68.1 %copy-start.9 = (bf16[1,512,128]{2,1,0:T(8,128)(2,1)S(1)}, bf16[1,512,128]{2,1,0:T(8,128)(2,1)}, u32[]{:S(2)}) copy-start(bf16[1,512,128]{2,1,0:T(8,128)(2,1)} %param.14) | copy-start | bytes 393220
  15.3 69.2 %copy-start = (bf16[1,320,512]{2,1,0:T(8,128)(2,1)S(1)}, bf16[1,320,512]{2,1,0:T(8,128)(2,1)}, u32[]{:S(2)}) copy-start(bf16[1,320,512]{2,1,0:T(8,128)(2,1)} %param.12) | copy-start | bytes 983044
  15.3 250.2 %all-gather.15.cloned.1.call-start = ((), (), s32[]{:S(2)}) async-start(), calls=%async_computation.3 | async-start | bytes 5406720 | tf_op jit(solution)/shard_map/all_gather | solution.py:97
  83.3 83.7 %copy-start.3 = (bf16[320,512]{1,0:T(8,128)(2,1)}, bf16[320,512]{1,0:T(8,128)(2,1)S(1)}, u32[]{:S(2)}) copy-start(bf16[320,512]{1,0:T(8,128)(2,1)S(1)} %fusion.131) | copy-start | bytes 983044
  83.3 81.4 %copy-start.10 = (f32[1,5,512]{2,0,1:T(1,128)S(1)}, f32[1,5,512]{2,0,1:T(1,128)}, u32[]{:S(2)}) copy-start(f32[1,5,512]{2,0,1:T(1,128)} %param.15) | copy-start | bytes 30724
  83.3 81.6 %copy-start.11 = (f32[5]{0:T(128)S(1)}, f32[5]{0:T(128)}, u32[]{:S(2)}) copy-start(f32[5]{0:T(128)} %param.17) | copy-start | bytes 64
  191.2 3.7 copy-start.1
  194.9 0.8 copy-start.2
  202.8 3.6 copy-start.1
  206.4 0.8 copy-start.2
  211.3 5.4 copy-start.5
  322.0 1.7 copy-start.4
  322.0 2.7 copy-start.12
  323.8 293.0 %copy-start.6 = (f32[2,256,128]{2,1,0:T(8,128)S(1)}, f32[2,256,128]{2,1,0:T(8,128)}, u32[]{:S(2)}) copy-start(f32[2,256,128]{2,1,0:T(8,128)} %get-tuple-element.972) | copy-start | bytes 786436
  323.8 293.0 %copy-start.7 = (f32[2,256,128]{2,1,0:T(8,128)S(1)}, f32[2,256,128]{2,1,0:T(8,128)}, u32[]{:S(2)}) copy-start(f32[2,256,128]{2,1,0:T(8,128)} %get-tuple-element.973) | copy-start | bytes 786436
Sparse Core Ops, SparseCore 0:
  10.1 22.5 all-gather.8
  34.7 45.2 all-gather.12
  83.8 90.8 all-gather.10
  177.7 87.8 all-gather.14
where the time goes:
time: 660 us; the launch traced here: 659 us
  blocking collectives  403 us (61%)
  waiting for transfers between devices  121 us (18%)
  matrix products  63.7 us (10%)
  other arithmetic  33.6 us (5%)
  local copies, waits for them, and re-layouts  21.4 us (3%)
  between operations  15.6 us (2%)
    psum x1, blocking collectives, per_device(): grad_alog, grad_skip = lax.psum((grads[4], grads[5]), ('seq', 'dp'))  291 us
    unnamed x1, blocking collectives  76.9 us
    all_gather x1, waiting for transfers between devices, per_device(): shard_part = lax.all_gather(local_cotan[None], 'seq', axis=0, tiled=True)  48 us
    all_gather x1, waiting for transfers between devices, per_device(): g_full = lax.all_gather(out_grad[0], 'tensor', axis=0, tiled=True)  47.4 us
    psum x1, blocking collectives, per_device(): grad_b, grad_c = lax.psum((grads[1], grads[2]), 'tensor')  35.5 us
    dot_general x6, matrix products, span_pass(): block_out = jnp.einsum('hps,hts->hpt', x_block, scores, precision=HIGH)  18.5 us
    another operation x23, other arithmetic  17.6 us
    all_gather x1, waiting for transfers between devices, per_device(): lax.all_gather(w_out, 'dp', axis=1, tiled=True)  17.3 us
  transfers between devices with their start and end apart: 4, of which 4 were waited for; matrix products, arithmetic and copies ran while one was open for 9% of the time, Pallas kernels for 0%

commit v1 on v0

--- a/solution.py
+++ b/solution.py
@@ -81,7 +81,9 @@
 
     primal, pullback = jax.vjp(local_sweep, streams, b_rows, c_rows, dt_rows, a_log, d_skip)
     mixed_half = primal[0].reshape(head_count * head_width, length).astype(jnp.bfloat16)
-    g_full = lax.all_gather(out_grad[0], "tensor", axis=0, tiled=True)
+    own = out_grad[0]
+    outgoing = jnp.stack([own] * lax.axis_size("tensor"))
+    g_full = jnp.concatenate(lax.all_to_all(outgoing, "tensor", 0, 0), axis=0)
     cotan_sum = jnp.dot(
         lax.all_gather(w_out, "dp", axis=1, tiled=True), g_full, preferred_element_type=jnp.float32
     )

time: 660 us -> 617 us (0.935)
  the two profiles are of different devices: /device:TPU:16 before, /device:TPU:8 now
where the time goes in v1:
time: 617 us; the launch traced here: 616 us
  blocking collectives  406 us (66%)
  matrix products  63.7 us (10%)
  waiting for transfers between devices  59.3 us (10%)
  other arithmetic  37.5 us (6%)
  local copies, waits for them, and re-layouts  23.6 us (4%)
  between operations  15.5 us (3%)
  starting transfers between devices  10.2 us (2%)
    psum x1, blocking collectives, per_device(): grad_alog, grad_skip = lax.psum((grads[4], grads[5]), ('seq', 'dp'))  291 us
    unnamed x1, blocking collectives  81.4 us
    all_to_all x1, waiting for transfers between devices, per_device(): g_full = jnp.concatenate(lax.all_to_all(outgoing, 'tensor', 0, 0), axis=0)  52.2 us
    psum x1, blocking collectives, per_device(): grad_b, grad_c = lax.psum((grads[1], grads[2]), 'tensor')  34.1 us
    dot_general x6, matrix products, span_pass(): block_out = jnp.einsum('hps,hts->hpt', x_block, scores, precision=HIGH)  18.5 us
    another operation x23, other arithmetic  17.6 us
  transfers between devices with their start and end apart: 4, of which 2 were waited for; matrix products, arithmetic and copies ran while one was open for 10% of the time, Pallas kernels for 0%

profile of v1, /device:TPU:8, one launch (start us, length us, event | category | flops | bytes accessed | tf_op | source)
XLA Modules:
  0.0 615.9 jit_solution(12326886181294547622)
XLA Ops:
  9.4 1.5 reduce-window.46
  12.4 1.1 bitcast_multiply_fusion.15
  13.4 1.1 fusion.131
  14.6 1.7 stack.3
  16.3 10.1 %all-to-all-start = ((bf16[8,320,512]{2,1,0:T(8,128)(2,1)}), bf16[8,320,512]{2,1,0:T(8,128)(2,1)}, u32[]{:S(2)}, u32[]{:S(2)}) async-start(bf16[8,320,512]{2,1,0:T(8,128)(2,1)} %stack.3), calls=%async_computation | async-start | bytes 5242880 | tf_op jit(solution)/shard_map/all_to_all | solution.py:86
  26.4 6.3 %all-gather.7.cloned.1.call-done = bf16[320,2560]{1,0:T(8,128)(2,1)} async-done(((bf16[320,1280]{1,0:T(8,128)(2,1)}), bf16[320,2560]{1,0:T(8,128)(2,1)}) %all-gather.7.cloned.1.call-update) | async-done | bytes 1638416 | tf_op jit(solution)/shard_map/all_gather | solution.py:88
  32.7 52.2 %all-to-all-done = bf16[8,320,512]{2,1,0:T(8,128)(2,1)} async-done(((bf16[8,320,512]{2,1,0:T(8,128)(2,1)}), bf16[8,320,512]{2,1,0:T(8,128)(2,1)}, u32[]{:S(2)}, u32[]{:S(2)}) %all-to-all-start) | async-done | bytes 2621472 | tf_op jit(solution)/shard_map/all_to_all | solution.py:86
  85.0 3.3 convolution_convert_fusion
  88.4 1.1 fusion.129
  90.1 1.3 dynamic-slice
  92.3 81.4 %all-reduce.2 = f32[160]{0:T(256)S(1)} all-reduce(f32[160]{0:T(256)S(1)} %dynamic-update-slice), channel_id=2, replica_groups=mesh['seq'=32,'dp'=2,'tensor'=8] {'seq'}, use_global_device_ids=true, to_apply=%add.2 | all-reduce | flops 160 | bytes 1280
  174.5 1.3 dynamic-slice.1
  176.4 1.2 reshape_reshape.4
  177.7 1.1 copy.169
  178.9 7.7 %fusion.125 = f32[5,1,64,128]{3,1,2,0:T(1,128)S(1)} fusion(f32[32,5,1,1]{0,2,3,1:T(1,128)S(1)} %copy.121, f32[32,5,64,128]{3,2,1,0:T(8,128)} %bitcast.480), kind=kOutput, calls=%fused_computation.159 | convolution fusion | flops 15728640 | bytes 5407360 | tf_op jit(solution)/shard_map/jh,jhpn->hpn/dot_general | solution.py:77
  189.3 24.0 %while.75 = (s32[]{:T(128)}, f32[5,64,128]{2,1,0:T(8,128)S(1)}, f32[2,5,64,256]{3,2,1,0:T(8,128)}, f32[2,5,256,256]{3,2,1,0:T(8,128)}, f32[2,128,256]{1,2,0:T(8,...) while((s32[]{:T(128)}, f32[5,64,128]{2,1,0:T(8,128)S(1)}, ...), condition=%wide.region_6.7_spmd.clone.clone, body=%wide.region_3.6_spmd.clone.clone.sunk | while | flops 607838976 | bytes 10914297 | solution.py:45
  189.4 1.5 reduce-window.60
  191.3 1.1 bitcast_dynamic-update-slice_fusion.11
  192.4 2.8 multiply_dynamic-update-slice_fusion.4
  195.5 1.2 bitcast_dynamic-update-slice_fusion.12
  196.6 2.4 fusion.205
  201.4 1.5 reduce-window.60
  203.3 1.1 bitcast_dynamic-update-slice_fusion.11
  204.4 2.9 multiply_dynamic-update-slice_fusion.4
  207.5 1.2 bitcast_dynamic-update-slice_fusion.12
  208.7 2.4 fusion.205
  213.3 1.3 add_convert_fusion
  215.0 5.3 fusion.145
  220.8 1.4 reshape.731
  222.2 2.0 add_convert_fusion.2
  224.1 7.7 %fusion.123 = f32[5,1,64,128]{3,1,2,0:T(1,128)S(1)} fusion(f32[32,5,1,1]{0,2,3,1:T(1,128)S(1)} %copy.124, f32[32,5,64,128]{3,2,1,0:T(8,128)} %bitcast.479), kind=kOutput, calls=%fused_computation.157 | convolution fusion | flops 15728640 | bytes 5407360 | tf_op jit(solution)/shard_map/jh,jhpn->hpn/dot_general | solution.py:107
  234.3 46.3 %while.76 = (s32[]{:T(128)}, f32[5]{0:T(128)S(1)}, f32[5,64,128]{2,1,0:T(8,128)S(1)}, f32[2,5,64,256]{3,2,1,0:T(8,128)}, f32[2,256,128]{2,1,0:T(8,128)}, /*index...) while((s32[]{:T(128)}, f32[5]{0:T(128)S(1)}, ...), condition=%wide.region_19.20_spmd.clone.clone, body=%wide.region_7.19_spmd.clone.clone.sunk | while | flops 1212566272 | bytes 13529267 | solution.py:45
  235.3 3.9 fusion.220
  240.2 1.0 fusion.221
  241.3 6.3 %reduce-window.62 = f32[5,2,128]{2,1,0:T(2,128)S(1)} reduce-window(f32[5,2,128]{2,1,0:T(2,128)S(1)} %reshape.778, f32[]{:T(128)} %constant.173.clone.1..sunk.1), window={size=1x1x128 pad=0_0x0_0x0_127}, to_apply=%region_14.14 | reduce-window | flops 162560 | bytes 10244 | tf_op jit(solution)/shard_map/reduce-window.20
  248.8 1.9 fusion.233
  251.0 1.8 convolution_bitcast_fusion.5
  252.7 1.3 fusion.232
  254.0 2.9 fusion.231
  258.4 3.9 fusion.220
  264.4 6.3 %reduce-window.62 = f32[5,2,128]{2,1,0:T(2,128)S(1)} reduce-window(f32[5,2,128]{2,1,0:T(2,128)S(1)} %reshape.778, f32[]{:T(128)} %constant.173.clone.1..sunk.1), window={size=1x1x128 pad=0_0x0_0x0_127}, to_apply=%region_14.14 | reduce-window | flops 162560 | bytes 10244 | tf_op jit(solution)/shard_map/reduce-window.20
  272.0 1.9 fusion.233
  274.1 1.8 convolution_bitcast_fusion.5
  275.9 1.2 fusion.232
  277.1 3.0 fusion.231
  280.6 1.6 copy.117
  284.2 290.5 %all-reduce.8 = (f32[5]{0:T(128)}, f32[5]{0:T(128)}, bf16[320,2560]{0,1:T(8,128)(2,1)S(1)}) all-reduce(f32[5]{0:T(128)S(1)} %negate_multiply_fusion, f32[5]{0:T(128)S(1)} %reduce_sum.212, f32[320,2560]{0,1:T(8,128)} %fusion.145), channel_id=1, replica_groups=mesh['seq'=32,'dp'=2,'tensor'=8] {'seq','dp'}, use_global_device_ids=true, to_apply=%region_22.23 | all-reduce | flops 819210 | bytes 4915280 | tf_op jit(solution)/shard_map/psum | solution.py:116
  575.3 34.1 %all-reduce.9 = (bf16[512,128]{1,0:T(8,128)(2,1)}, bf16[512,128]{1,0:T(8,128)(2,1)}) all-reduce(f32[512,128]{1,0:T(8,128)S(1)} %bitcast.495, f32[512,128]{1,0:T(8,128)S(1)} %bitcast.496), channel_id=1, replica_groups=mesh['seq'=32,'dp'=2,'tensor'=8] {'tensor'}, use_global_device_ids=true, to_apply=%region_20.21 | all-reduce | flops 131072 | bytes 786432 | tf_op jit(solution)/shard_map/psum | solution.py:115
  (206 shorter events, 28.6 us)
Async XLA Ops:
  7.2 6.3 %copy-start.7 = (bf16[1,512,128]{2,1,0:T(8,128)(2,1)S(1)}, bf16[1,512,128]{2,1,0:T(8,128)(2,1)}, u32[]{:S(2)}) copy-start(bf16[1,512,128]{2,1,0:T(8,128)(2,1)} %param.13) | copy-start | bytes 393220
  7.2 7.4 %copy-start.9 = (bf16[1,320,512]{2,1,0:T(8,128)(2,1)S(1)}, bf16[1,320,512]{2,1,0:T(8,128)(2,1)}, u32[]{:S(2)}) copy-start(bf16[1,320,512]{2,1,0:T(8,128)(2,1)} %param.19) | copy-start | bytes 983044
  7.2 25.6 %all-gather.7.cloned.1.call-start = ((), (), s32[]{:S(2)}) async-start(), calls=%async_computation.1 | async-start | bytes 2457600 | tf_op jit(solution)/shard_map/all_gather | solution.py:88
  7.9 170.9 %all-gather.9.cloned.1.call-start = ((), (), s32[]{:S(2)}) async-start(), calls=%async_computation.2 | async-start | bytes 5406720 | tf_op jit(solution)/shard_map/all_gather | solution.py:71
  16.3 68.6 %all-to-all-start = ((bf16[8,320,512]{2,1,0:T(8,128)(2,1)}), bf16[8,320,512]{2,1,0:T(8,128)(2,1)}, u32[]{:S(2)}, u32[]{:S(2)}) async-start(bf16[8,320,512]{2,1,0:T(8,128)(2,1)} %stack.3), calls=%async_computation | async-start | bytes 5242880 | tf_op jit(solution)/shard_map/all_to_all | solution.py:86
  26.4 197.7 %all-gather.11.cloned.1.call-start = ((), (), s32[]{:S(2)}) async-start(), calls=%async_computation.3 | async-start | bytes 5406720 | tf_op jit(solution)/shard_map/all_gather | solution.py:99
  85.0 3.4 copy-start.8
  85.0 4.6 copy-start.1
  88.3 88.2 %copy-start.3 = (bf16[320,512]{1,0:T(8,128)(2,1)}, bf16[320,512]{1,0:T(8,128)(2,1)S(1)}, u32[]{:S(2)}) copy-start(bf16[320,512]{1,0:T(8,128)(2,1)S(1)} %convolution_convert_fusion) | copy-start | bytes 983044
  88.3 85.9 %copy-start.10 = (f32[1,5,512]{2,0,1:T(1,128)S(1)}, f32[1,5,512]{2,0,1:T(1,128)}, u32[]{:S(2)}) copy-start(f32[1,5,512]{2,0,1:T(1,128)} %param.15) | copy-start | bytes 30724
  88.3 86.1 %copy-start.11 = (f32[5]{0:T(128)S(1)}, f32[5]{0:T(128)}, u32[]{:S(2)}) copy-start(f32[5]{0:T(128)} %param.17) | copy-start | bytes 64
  215.0 5.3 copy-start
  220.3 1.9 copy-start.2
  280.6 1.7 copy-start.4
  280.6 2.7 copy-start.12
  282.3 293.0 %copy-start.5 = (f32[2,256,128]{2,1,0:T(8,128)S(1)}, f32[2,256,128]{2,1,0:T(8,128)}, u32[]{:S(2)}) copy-start(f32[2,256,128]{2,1,0:T(8,128)} %get-tuple-element.972) | copy-start | bytes 786436
  282.3 293.0 %copy-start.6 = (f32[2,256,128]{2,1,0:T(8,128)S(1)}, f32[2,256,128]{2,1,0:T(8,128)}, u32[]{:S(2)}) copy-start(f32[2,256,128]{2,1,0:T(8,128)} %get-tuple-element.973) | copy-start | bytes 786436
Sparse Core Ops, SparseCore 0:
  10.1 22.5 all-gather.6
  36.5 92.1 all-gather.8
  131.9 87.5 all-gather.10
